TPU v7x, 32 devices: a whole 2x2x4 slice. The times are simulated.
32 devices in a mesh: seq: 16 (over z, y, x), chan: 2 (over core).
Axes of the slice: x: 2, y: 2, z: 4, core: 2. Of those that a mesh axis runs over, the one named last changes fastest.
Arguments:
- tokens: bfloat16 [2048, 4096], P('seq', 'chan'), may hold values from -6 to 6
- conv_taps: float32 [4, 4096], P(None, 'chan'), may hold values from -12 to 12
- log_rate: float32 [4096], P('chan'), may hold values from 1.953125e-05 to 0.034
- rotation: float32 [4096], P('chan'), may hold values from 0 to 0.2
- in_proj: bfloat16 [64, 64, 128], P('chan'), may hold values from -0.75 to 0.75
- out_proj: bfloat16 [64, 64, 128], P('chan'), may hold values from -0.5 to 0.5
- skip_gain: float32 [4096], P('chan'), may hold values from 0.25 to 1.5
- norm_gain: float32 [4096], P('chan'), may hold values from 0.25 to 1.75
- retention: float32 [2048], P('seq'), may hold values from 0.5 to 1
- cotangent: bfloat16 [2048, 4096], P('seq', 'chan'), may hold values from -6 to 6
Outputs:
- normed: bfloat16 [2048, 4096], P('seq', 'chan')
- tokens_grad: bfloat16 [2048, 4096], P('seq', 'chan')
- in_grad: float32 [64, 64, 128], P('chan')
- out_grad: float32 [64, 64, 128], P('chan')
- taps_grad: float32 [4, 4096], P(None, 'chan')
All inputs are finite; a program needn't handle non-finite values.
Results may differ from a plain program's by a relative error of at most 0.011.
Values may be sent and summed in bfloat16 or wider, within the bound.
A program may use at most 128 MiB of HBM per device.

v0:
```python
import jax
import jax.numpy as jnp
from jax import lax
from jax.sharding import PartitionSpec as P


def from_behind(value, axis, by):
    length = lax.axis_size(axis)
    pairs = [(i, i + by) for i in range(length) if 0 <= i + by < length]
    return lax.ppermute(value, axis, pairs)


def carried_in(part, axis, combine, identity, reverse):
    count = lax.axis_size(axis)
    place = lax.axis_index(axis)
    ahead = count - 1 - place if reverse else place
    gathered = jax.tree.map(lambda a: lax.all_gather(a, axis), part)
    state = jax.tree.map(lambda a, e: jnp.zeros_like(a) + jnp.asarray(e, a.dtype), part, identity)

    def one(hop, state):
        source = count - 1 - hop if reverse else hop
        return combine(
            state, jax.tree.map(lambda a: lax.dynamic_index_in_dim(a, source, 0, False), gathered)
        )

    return lax.fori_loop(0, ahead, one, state)


def linear_run(drive_re, drive_im, decay_rate, turn_rate, log_keep):
    seq_len, num_cols = drive_re.shape
    block_len = min(64, seq_len)
    block_count = seq_len // block_len
    offsets = jnp.arange(block_len, dtype=jnp.float32)
    keep_cum = jnp.cumsum(log_keep.reshape(block_count, block_len), axis=1)[:, :, None]
    angles = offsets[:, None] * turn_rate[None, :]
    cosine = jnp.cos(angles)
    sine = jnp.sin(angles)
    growth = jnp.exp(offsets[None, :, None] * decay_rate[None, None, :] - keep_cum)
    blk_re = drive_re.reshape(block_count, block_len, num_cols)
    blk_im = drive_im.reshape(block_count, block_len, num_cols)
    pre_re = growth * (blk_re * cosine + blk_im * sine)
    pre_im = growth * (blk_im * cosine - blk_re * sine)
    lower_ones = (offsets[:, None] >= offsets[None, :]).astype(jnp.float32)
    summed = jnp.einsum(
        "ji,abik->abjk", lower_ones, jnp.stack([pre_re, pre_im]), precision=lax.Precision.HIGHEST
    )
    shrink = jnp.exp(keep_cum - offsets[None, :, None] * decay_rate[None, None, :])
    state_re = shrink * (summed[0] * cosine - summed[1] * sine)
    state_im = shrink * (summed[0] * sine + summed[1] * cosine)
    step_mag = jnp.exp(keep_cum[:, -1] - block_len * decay_rate[None, :])
    step_re = step_mag * jnp.cos(block_len * turn_rate)[None, :]
    step_im = step_mag * jnp.sin(block_len * turn_rate)[None, :]

    def advance(carried, inputs):
        carry_re, carry_im = carried
        mult_re, mult_im, end_re, end_im = inputs
        next_re = mult_re * carry_re - mult_im * carry_im + end_re
        next_im = mult_re * carry_im + mult_im * carry_re + end_im
        return ((next_re, next_im), (carry_re, carry_im))

    zeros_col = jnp.zeros((num_cols,), jnp.float32)
    enter_re, enter_im = lax.scan(
        advance, (zeros_col, zeros_col), (step_re, step_im, state_re[:, -1], state_im[:, -1])
    )[1]
    ahead = offsets + 1.0
    lift = jnp.exp(keep_cum - ahead[None, :, None] * decay_rate[None, None, :])
    lift_re = lift * jnp.cos(ahead[:, None] * turn_rate[None, :])
    lift_im = lift * jnp.sin(ahead[:, None] * turn_rate[None, :])
    state_re = state_re + lift_re * enter_re[:, None] - lift_im * enter_im[:, None]
    state_im = state_im + lift_re * enter_im[:, None] + lift_im * enter_re[:, None]
    return (state_re.reshape(seq_len, num_cols), state_im.reshape(seq_len, num_cols))


def carry_combine(earlier, later):
    early_re, early_im, early_sre, early_sim = earlier
    late_re, late_im, late_sre, late_sim = later
    joined_re = early_re * late_re - early_im * late_im
    joined_im = early_re * late_im + early_im * late_re
    joined_sre = late_re * early_sre - late_im * early_sim + late_sre
    joined_sim = late_re * early_sim + late_im * early_sre + late_sim
    return (joined_re, joined_im, joined_sre, joined_sim)


def per_device(
    tokens,
    conv_taps,
    log_rate,
    rotation,
    in_proj,
    out_proj,
    skip_gain,
    norm_gain,
    retention,
    cotangent,
):
    seq_len, local_width = tokens.shape
    tap_count = conv_taps.shape[0]
    local_heads, head_width, double_state = in_proj.shape
    state_size = double_state // 2
    num_cols = local_heads * state_size
    lead_rows = from_behind(tokens[seq_len - (tap_count - 1) :], "seq", 1)
    padded = jnp.concatenate([lead_rows, tokens], axis=0).astype(jnp.float32)
    conv_sum = conv_taps[0][None, :] * padded[tap_count - 1 :]
    for offset in range(1, tap_count):
        conv_sum = (
            conv_sum
            + conv_taps[offset][None, :]
            * padded[tap_count - 1 - offset : tap_count - 1 - offset + seq_len]
        )
    mixed_in = conv_sum.astype(jnp.bfloat16)
    by_head = mixed_in.reshape(seq_len, local_heads, head_width)
    projected = jnp.einsum("thc,hck->thk", by_head, in_proj, preferred_element_type=jnp.float32)
    in_scale = jnp.sqrt(-jnp.expm1(-2.0 * log_rate))
    drive_re = projected[:, :, :state_size].reshape(seq_len, num_cols) * in_scale
    drive_im = projected[:, :, state_size:].reshape(seq_len, num_cols) * in_scale
    log_keep = jnp.log(retention)
    state_re, state_im = linear_run(drive_re, drive_im, log_rate, rotation, log_keep)
    keep_total = jnp.sum(log_keep)
    total_mag = jnp.exp(keep_total - seq_len * log_rate)
    total_re = total_mag * jnp.cos(seq_len * rotation)
    total_im = total_mag * jnp.sin(seq_len * rotation)
    unit_ones = jnp.ones((num_cols,), jnp.float32)
    zeros_col = jnp.zeros((num_cols,), jnp.float32)
    chained = carried_in(
        (total_re, total_im, state_re[-1], state_im[-1]),
        "seq",
        carry_combine,
        (unit_ones, zeros_col, zeros_col, zeros_col),
        False,
    )
    enter_re, enter_im = (chained[2], chained[3])
    positions = jnp.arange(seq_len, dtype=jnp.float32)
    ahead = positions + 1.0
    lift = jnp.exp(jnp.cumsum(log_keep)[:, None] - ahead[:, None] * log_rate[None, :])
    lift_re = lift * jnp.cos(ahead[:, None] * rotation[None, :])
    lift_im = lift * jnp.sin(ahead[:, None] * rotation[None, :])
    state_re = state_re + lift_re * enter_re[None, :] - lift_im * enter_im[None, :]
    state_im = state_im + lift_re * enter_im[None, :] + lift_im * enter_re[None, :]
    state_bf = jnp.concatenate(
        [
            state_re.reshape(seq_len, local_heads, state_size),
            state_im.reshape(seq_len, local_heads, state_size),
        ],
        axis=2,
    ).astype(jnp.bfloat16)
    mixed = jnp.einsum(
        "thk,hck->thc", state_bf, out_proj, preferred_element_type=jnp.float32
    ).reshape(seq_len, local_width)
    mixed = mixed + skip_gain * mixed_in.astype(jnp.float32)
    squares = jnp.sum(mixed * mixed, axis=1)
    scaled = cotangent.astype(jnp.float32) * norm_gain
    dots = jnp.sum(scaled * mixed, axis=1)
    squares = lax.psum(squares, "chan")
    model_width = local_width * lax.axis_size("chan")
    inverse = lax.rsqrt(squares / model_width + 1e-06)
    normed = (mixed * inverse[:, None] * norm_gain).astype(jnp.bfloat16)
    dots = lax.psum(dots, "chan")
    mixed_grad = inverse[:, None] * (
        scaled - mixed * (inverse * inverse * dots / model_width)[:, None]
    )
    grad_bf = mixed_grad.astype(jnp.bfloat16).reshape(seq_len, local_heads, head_width)
    state_grad = jnp.einsum("thc,hck->thk", grad_bf, out_proj, preferred_element_type=jnp.float32)
    out_grad = jnp.einsum("thc,thk->hck", grad_bf, state_bf, preferred_element_type=jnp.float32)
    back_keep = jnp.concatenate([jnp.zeros((1,), jnp.float32), log_keep[::-1][:-1]])
    grad_re = state_grad[:, :, :state_size].reshape(seq_len, num_cols)[::-1]
    grad_im = state_grad[:, :, state_size:].reshape(seq_len, num_cols)[::-1]
    adj_re, adj_im = linear_run(grad_re, grad_im, log_rate, -rotation, back_keep)
    first_mag = jnp.exp(log_keep[0] - log_rate)
    cos_turn = jnp.cos(rotation)
    sin_turn = jnp.sin(rotation)
    first_re = first_mag * (cos_turn * adj_re[-1] + sin_turn * adj_im[-1])
    first_im = first_mag * (cos_turn * adj_im[-1] - sin_turn * adj_re[-1])
    back_chained = carried_in(
        (total_re, -total_im, first_re, first_im),
        "seq",
        carry_combine,
        (unit_ones, zeros_col, zeros_col, zeros_col),
        True,
    )
    later_re, later_im = (back_chained[2], back_chained[3])
    back_lift = jnp.exp(jnp.cumsum(back_keep)[:, None] - positions[:, None] * log_rate[None, :])
    back_re = back_lift * jnp.cos(positions[:, None] * rotation[None, :])
    back_im = -back_lift * jnp.sin(positions[:, None] * rotation[None, :])
    adj_re = adj_re + back_re * later_re[None, :] - back_im * later_im[None, :]
    adj_im = adj_im + back_re * later_im[None, :] + back_im * later_re[None, :]
    adj_re = adj_re[::-1]
    adj_im = adj_im[::-1]
    drive_grad = jnp.concatenate(
        [
            (in_scale * adj_re).reshape(seq_len, local_heads, state_size),
            (in_scale * adj_im).reshape(seq_len, local_heads, state_size),
        ],
        axis=2,
    ).astype(jnp.bfloat16)
    in_grad = jnp.einsum("thc,thk->hck", by_head, drive_grad, preferred_element_type=jnp.float32)
    input_grad = jnp.einsum(
        "thk,hck->thc", drive_grad, in_proj, preferred_element_type=jnp.float32
    ).reshape(seq_len, local_width)
    input_grad = input_grad + skip_gain * mixed_grad
    trail_rows = from_behind(input_grad[: tap_count - 1], "seq", -1)
    tail = jnp.concatenate([input_grad, trail_rows], axis=0)
    tokens_grad = conv_taps[0][None, :] * tail[:seq_len]
    for offset in range(1, tap_count):
        tokens_grad = tokens_grad + conv_taps[offset][None, :] * tail[offset : offset + seq_len]
    taps_grad = jnp.stack(
        [
            jnp.sum(
                input_grad * padded[tap_count - 1 - offset : tap_count - 1 - offset + seq_len],
                axis=0,
            )
            for offset in range(tap_count)
        ]
    )
    in_grad, out_grad, taps_grad = lax.psum((in_grad, out_grad, taps_grad), "seq")
    return (normed, tokens_grad.astype(jnp.bfloat16), in_grad, out_grad, taps_grad)


def solution(mesh):
    in_specs = (
        P("seq", "chan"),
        P(None, "chan"),
        P("chan"),
        P("chan"),
        P("chan", None, None),
        P("chan", None, None),
        P("chan"),
        P("chan"),
        P("seq"),
        P("seq", "chan"),
    )
    out_specs = (
        P("seq", "chan"),
        P("seq", "chan"),
        P("chan", None, None),
        P("chan", None, None),
        P(None, "chan"),
    )
    return jax.shard_map(
        per_device, mesh=mesh, in_specs=in_specs, out_specs=out_specs, check_vma=False
    )
```

profile of v0, /device:TPU:0, one launch (start us, length us, event | category | flops | bytes accessed | tf_op | source)
XLA Modules:
  0.0 679.5 jit_solution(8325119670309983205)
XLA Ops:
  9.1 5.6 collective-permute-start
  21.9 38.8 %all-gather = f32[32768]{0:T(1024)S(1)} all-gather(f32[2048]{0:T(1024)S(1)} %get-tuple-element.552), channel_id=2, replica_groups=mesh['seq'=16,'chan'=2] {'seq'}, dimensions={0}, use_global_device_ids=true | all-gather | bytes 139264 | tf_op jit(solution)/shard_map/all_gather | solution.py:17
  60.7 36.1 %all-gather.1 = f32[32768]{0:T(1024)S(1)} all-gather(f32[2048]{0:T(1024)S(1)} %get-tuple-element.554), channel_id=3, replica_groups=mesh['seq'=16,'chan'=2] {'seq'}, dimensions={0}, use_global_device_ids=true | all-gather | bytes 139264 | tf_op jit(solution)/shard_map/all_gather | solution.py:17
  96.9 9.7 %multiply_cosine_fusion.1 = (f32[64,2048]{1,0:T(8,128)}, f32[64,2048]{1,0:T(8,128)}, f32[64,2048]{1,0:T(8,128)}, f32[64,2048]{1,0:T(8,128)}, f32[64,2048]{1,0:T(...) fusion(f32[2048]{0:T(1024)S(1)} %get-tuple-element.557, ...), kind=kLoop, calls=%fused_computation.123 | loop fusion | flops 786432 | bytes 5267712 | tf_op jit(solution)/shard_map/cos | solution.py:67
  109.0 38.7 %all-gather.2 = f32[32768]{0:T(1024)S(1)} all-gather(f32[2048]{0:T(1024)S(1)} %get-tuple-element.553), channel_id=4, replica_groups=mesh['seq'=16,'chan'=2] {'seq'}, dimensions={0}, use_global_device_ids=true | all-gather | bytes 139264 | tf_op jit(solution)/shard_map/all_gather | solution.py:17
  183.8 3.3 fusion.18
  206.9 3.4 reshape.696
  210.2 3.9 copy.204
  214.2 3.4 reshape.697
  217.5 3.9 copy.205
  229.1 5.6 while.68
  243.7 3.2 squeeze.124
  251.2 36.2 %all-gather.6 = f32[16,1,2048]{2,1,0:T(1,128)S(1)} all-gather(f32[1,1,2048]{2,1,0:T(1,128)S(1)} %get-tuple-element.500), channel_id=1, replica_groups=mesh['seq'=16,'chan'=2] {'seq'}, dimensions={0}, use_global_device_ids=true | all-gather | bytes 139264 | tf_op jit(solution)/shard_map/all_gather | solution.py:17
  288.0 38.2 %all-gather.5 = f32[16,1,2048]{2,1,0:T(1,128)S(1)} all-gather(f32[1,1,2048]{2,1,0:T(1,128)S(1)} %get-tuple-element.501), channel_id=1, replica_groups=mesh['seq'=16,'chan'=2] {'seq'}, dimensions={0}, use_global_device_ids=true | all-gather | bytes 139264 | tf_op jit(solution)/shard_map/all_gather | solution.py:17
  327.1 3.7 copy.176
  330.8 3.6 copy.178
  334.4 3.7 copy.170
  338.1 3.7 copy.172
  341.8 9.2 %subtract_convert_fusion = (bf16[128,32,64]{0,2,1:T(8,128)(2,1)S(1)}, bf16[128,32,64]{0,2,1:T(8,128)(2,1)S(1)}) fusion(f32[128,32,64]{0,2,1:T(8,128)} %copy.178, f32[128,32,64]{0,2,1:T(8,128)} %copy.176, f32[128,32,64]{0,2,1:T(8,128)} %copy.172, f32[128,32,64]{0,2,1:T(8,128)} %copy.173, f32[128,32,64]{0,2,1:T(8,128)} %copy.170, f32[128,32,64]{0,2,1:T(8,128)} %copy.171, ...), kind=kLoop, calls=%fused_computation.111 | loop fusion | flops 9175040 | bytes 11568640 | tf_op jit(solution)/shard_map/convert.4
  352.4 3.6 multiply_reduce_fusion.4
  367.2 9.2 %rev.13 = f32[128,2048]{1,0:T(8,128)} reverse(f32[128,2048]{1,0:T(8,128)} %copy.189), dimensions={0} | reverse | bytes 2097152 | tf_op jit(solution)/shard_map/rev | solution.py:165
  378.9 9.0 %rev.14 = f32[128,2048]{1,0:T(8,128)} reverse(f32[128,2048]{1,0:T(8,128)} %copy.190), dimensions={0} | reverse | bytes 2097152 | tf_op jit(solution)/shard_map/rev | solution.py:166
  395.4 5.6 while.69
  401.0 3.3 fusion.13
  405.7 63.0 %all-gather.3 = f32[32768]{0:T(1024)S(1)} all-gather(f32[2048]{0:T(1024)S(1)} %get-tuple-element.530), channel_id=5, replica_groups=mesh['seq'=16,'chan'=2] {'seq'}, dimensions={0}, use_global_device_ids=true | all-gather | bytes 139264 | tf_op jit(solution)/shard_map/all_gather | solution.py:17
  468.8 36.1 %all-gather.4 = f32[32768]{0:T(1024)S(1)} all-gather(f32[2048]{0:T(1024)S(1)} %get-tuple-element.529), channel_id=6, replica_groups=mesh['seq'=16,'chan'=2] {'seq'}, dimensions={0}, use_global_device_ids=true | all-gather | bytes 139264 | tf_op jit(solution)/shard_map/all_gather | solution.py:17
  506.5 6.4 multiply_subtract_fusion
  512.9 9.0 %rev.15 = f32[128,2048]{1,0:T(8,128)} reverse(f32[128,2048]{1,0:T(8,128)} %get-tuple-element.531), dimensions={0} | reverse | bytes 2097152 | tf_op jit(solution)/shard_map/rev | solution.py:186
  521.8 8.9 %rev.16 = f32[128,2048]{1,0:T(8,128)} reverse(f32[128,2048]{1,0:T(8,128)} %get-tuple-element.532), dimensions={0} | reverse | bytes 2097152 | tf_op jit(solution)/shard_map/rev | solution.py:187
  548.0 3.6 multiply_reduce_fusion.3
  555.5 75.7 %psum.39 = f32[4,2048]{1,0:T(4,128)} all-reduce(f32[4,2048]{1,0:T(4,128)S(1)} %pad_maximum_fusion.7), channel_id=1, replica_groups=mesh['seq'=16,'chan'=2] {'seq'}, use_global_device_ids=true, to_apply=%region_23.24 | all-reduce | flops 8192 | bytes 65536 | tf_op jit(solution)/shard_map/psum | solution.py:214
  635.7 33.2 %all-reduce.4.cloned.1.call-done = (f32[32,64,128]{2,1,0:T(8,128)}, f32[32,64,128]{2,1,0:T(8,128)}) async-done(((f32[32,64,128]{2,1,0:T(8,128)}, f32[32,64,128]{2,1,0:T(8,128)}), (f32[32,64,128]{2,1,0:T(8,128)}, f32[32,64,128]{2,1,0:T(8,128)})) %all-reduce.4.cloned.1.call-update) | async-done | bytes 2097168 | tf_op jit(solution)/shard_map/psum | solution.py:214
  (332 shorter events, 155.8 us)
Async XLA Ops:
  7.2 344.7 %copy-start = (bf16[32,64,128]{2,1,0:T(8,128)(2,1)S(1)}, bf16[32,64,128]{2,1,0:T(8,128)(2,1)}, u32[]{:S(2)}) copy-start(bf16[32,64,128]{2,1,0:T(8,128)(2,1)} %param.23) | copy-start | bytes 1572868
  7.2 661.7 %all-reduce.4.cloned.1.call-start = ((), (), s32[]{:S(2)}) async-start(), calls=%async_computation | async-start | bytes 4194304 | tf_op jit(solution)/shard_map/psum | solution.py:214
  9.1 191.1 %collective-permute-start = (bf16[3,2048]{0,1:T(8,128)(2,1)}, bf16[3,2048]{0,1:T(8,128)(2,1)}, u32[]{:S(2)}, u32[]{:S(2)}) collective-permute-start(bf16[3,2048]{0,1:T(8,128)(2,1)} %copy.166), channel_id=1, source_target_pairs={{0,2},{2,4},{4,6},{6,8},{8,10},{10,12},{12,14},{14,16},{16,18},{18... | collective-permute-start | bytes 36872 | tf_op jit(solution)/shard_map/ppermute | solution.py:10
  17.4 131.3 %copy-start.54 = (f32[2,64]{1,0:T(2,128)}, f32[2,64]{1,0:T(2,128)S(1)}, u32[]{:S(2)}) copy-start(f32[2,64]{1,0:T(2,128)S(1)} %reduce) | copy-start | bytes 1540
  17.6 132.5 %copy-start.52 = (f32[2,64]{1,0:T(2,128)}, f32[2,64]{1,0:T(2,128)S(1)}, u32[]{:S(2)}) copy-start(f32[2,64]{1,0:T(2,128)S(1)} %reduce.4) | copy-start | bytes 1540
  106.6 45.5 %copy-start.5 = (f32[64,2048]{1,0:T(8,128)}, f32[64,2048]{1,0:T(8,128)S(1)}, u32[]{:S(2)}) copy-start(f32[64,2048]{1,0:T(8,128)S(1)} %get-tuple-element.570) | copy-start | bytes 1572868
  106.6 45.5 %copy-start.6 = (f32[64,2048]{1,0:T(8,128)}, f32[64,2048]{1,0:T(8,128)S(1)}, u32[]{:S(2)}) copy-start(f32[64,2048]{1,0:T(8,128)S(1)} %get-tuple-element.571) | copy-start | bytes 1572868
  106.6 41.1 %copy-start.19 = (bf16[128,2048]{1,0:T(8,128)(2,1)S(1)}, bf16[128,2048]{1,0:T(8,128)(2,1)}, u32[]{:S(2)}) copy-start(bf16[128,2048]{1,0:T(8,128)(2,1)} %param.18) | copy-start | bytes 1572868
  106.6 42.2 %copy-start.20 = (f32[2048]{0:T(1024)S(1)}, f32[2048]{0:T(1024)}, u32[]{:S(2)}) copy-start(f32[2048]{0:T(1024)} %param.20) | copy-start | bytes 24580
  106.6 42.8 %copy-start.28 = (f32[2048]{0:T(1024)S(1)}, f32[2048]{0:T(1024)}, u32[]{:S(2)}) copy-start(f32[2048]{0:T(1024)} %param.21) | copy-start | bytes 24580
  148.8 35.0 %copy-start.64 = (f32[128]{0:T(128)}, f32[128]{0:T(128)S(1)}, u32[]{:S(2)}) copy-start(f32[128]{0:T(128)S(1)} %sub.278) | copy-start | bytes 1540
  217.5 4.0 copy-start.37
  217.5 4.0 copy-start.55
  225.2 3.9 copy-start.22
  225.2 3.9 copy-start.23
  225.2 3.9 copy-start.26
  225.2 3.9 copy-start.27
  234.7 4.9 copy-start.43
  376.4 11.5 %copy-start.53 = (f32[2,64]{1,0:T(2,128)S(1)}, f32[2,64]{1,0:T(2,128)}, u32[]{:S(2)}) copy-start(f32[2,64]{1,0:T(2,128)} %copy-done.52) | copy-start | bytes 1540
  391.5 3.8 copy-start.21
  401.0 4.6 copy-start.44
  401.0 4.6 copy-start.45
  401.0 4.6 copy-start.57
  401.0 105.5 %copy-start.29 = (f32[2048]{0:T(1024)S(1)}, f32[2048]{0:T(1024)}, u32[]{:S(2)}) copy-start(f32[2048]{0:T(1024)} %param.21) | copy-start | bytes 24580
  401.0 105.5 %copy-start.62 = (f32[128]{0:T(128)S(1)}, f32[128]{0:T(128)}, u32[]{:S(2)}) copy-start(f32[128]{0:T(128)} %reduce.7) | copy-start | bytes 1540
  512.9 17.8 %copy-start.38 = (f32[2048]{0:T(1024)S(1)}, f32[2048]{0:T(1024)}, u32[]{:S(2)}) copy-start(f32[2048]{0:T(1024)} %get-tuple-element.556) | copy-start | bytes 24580
  534.2 6.8 %copy-start.12 = (bf16[128,2048]{0,1:T(8,128)(2,1)S(1)}, bf16[128,2048]{0,1:T(8,128)(2,1)}, u32[]{:S(2)}) copy-start(bf16[128,2048]{0,1:T(8,128)(2,1)} %copy-done.11) | copy-start | bytes 1572868
  551.5 80.1 %copy-start.1 = (f32[128,2048]{0,1:T(8,128)S(1)}, f32[128,2048]{0,1:T(8,128)}, u32[]{:S(2)}) copy-start(f32[128,2048]{0,1:T(8,128)} %get-tuple-element.474) | copy-start | bytes 3145732
  551.5 80.1 %copy-start.32 = (f32[1,2048]{1,0:T(1,128)S(1)}, f32[1,2048]{1,0:T(1,128)}, u32[]{:S(2)}) copy-start(f32[1,2048]{1,0:T(1,128)} %get-tuple-element.534) | copy-start | bytes 24580
  551.5 80.1 %copy-start.34 = (f32[1,2048]{1,0:T(1,128)S(1)}, f32[1,2048]{1,0:T(1,128)}, u32[]{:S(2)}) copy-start(f32[1,2048]{1,0:T(1,128)} %get-tuple-element.535) | copy-start | bytes 24580
  551.5 80.1 %copy-start.36 = (f32[1,2048]{1,0:T(1,128)S(1)}, f32[1,2048]{1,0:T(1,128)}, u32[]{:S(2)}) copy-start(f32[1,2048]{1,0:T(1,128)} %get-tuple-element.536) | copy-start | bytes 24580
  553.2 78.0 %collective-permute-start.1 = (f32[3,2048]{1,0:T(4,128)S(1)}, f32[3,2048]{1,0:T(4,128)S(1)}, u32[]{:S(2)}, u32[]{:S(2)}) collective-permute-start(f32[3,2048]{1,0:T(4,128)S(1)} %copy.196), channel_id=1, source_target_pairs={{2,0},{4,2},{6,4},{8,6},{10,8},{12,10},{14,12},{16,14},{18,16},{20... | collective-permute-start | bytes 73736 | tf_op jit(solution)/shard_map/ppermute | solution.py:10
  (38 other events, 81.7 us)
Sparse Core Ops, SparseCore 0:
  544.5 124.3 all-reduce.3
where the time goes:
time: 688 us; the launch traced here: 680 us
  blocking collectives  365 us (53%)
  local copies, waits for them, and re-layouts  178 us (26%)
  other arithmetic  68 us (10%)
  waiting for transfers between devices  33.2 us (5%)
  between operations  15.4 us (2%)
  matrix products  11.6 us (2%)
  starting transfers between devices  6.95 us (1%)
    all_gather x7, blocking collectives, carried_in(): gathered = jax.tree.map(lambda a: lax.all_gather(a, axis), part)  287 us
    psum x1, blocking collectives, per_device(): lax.psum((in_grad, out_grad, taps_grad), 'seq')  75.7 us
    psum x1, waiting for transfers between devices, per_device(): lax.psum((in_grad, out_grad, taps_grad), 'seq')  33.2 us
    another operation x8, other arithmetic  15.3 us
    squeeze x5, local copies, waits for them, and re-layouts, linear_run(): state_re = shrink * (summed[0] * cosine - summed[1] * sine)  15.2 us
    unnamed x145, local copies, waits for them, and re-layouts  14 us
  transfers between devices with their start and end apart: 3, of which 1 were waited for; matrix products, arithmetic and copies ran while one was open for 12% of the time, Pallas kernels for 0%

commit v1 on v0

v1 whole, which is shorter than its diff:
```python
import functools

import jax
import jax.numpy as jnp
from jax import lax
from jax.experimental import pallas as pl
from jax.experimental.pallas import tpu as pltpu
from jax.sharding import PartitionSpec as P

LANES = 128
F32 = jnp.float32
BF16 = jnp.bfloat16


def cmul(a, b):
    return a[0] * b[0] - a[1] * b[1], a[0] * b[1] + a[1] * b[0]


def cpow(base, exponent):
    result = None
    while exponent:
        if exponent & 1:
            result = base if result is None else cmul(result, base)
        exponent >>= 1
        if exponent:
            base = cmul(base, base)
    return result


def dot(a, b, ca, cb):
    return lax.dot_general(a, b, (((ca,), (cb,)), ((), ())), preferred_element_type=F32)


def scale_of(rate):
    sq = rate * rate
    sinh = rate * (1 + sq / 6 * (1 + sq / 20 * (1 + sq / 42 * (1 + sq / 72))))
    return jnp.sqrt(2.0 * jnp.exp(-rate) * sinh)


def kernel(dims, *refs):
    (tok, taps, rate_row, rate_t, rot_t, win, wout, skip, gain, cot, keep,
     normed_o, tg_o, in_o, out_o, taps_o,
     pad, mixed_in, d_re, d_im, s_bf, mixed, g_bf, ig, w_in, w_out, scale_row, tsc, halo, ihalo,
     nbuf, fb1, fb2, bb1, bb2, msg_o, rs1_o, mid_o, rs2_o, res_o,
     msg_i, rs1_i, mid_i, rs2_i, res_i,
     s_halo, s_norm, s_f1, s_f2, s_b1, s_b2, s_o1, s_o2, s_o3, s_o4, s_i1, s_i2, s_i3, s_i4) = refs
    T, W, NP, PP, KW, HW, G, Z, C, NSEQ, ROWS, RO, RI = dims
    me = lax.axis_index("seq")
    core = lax.axis_index("chan")
    gi = lax.rem(me, G)
    zi = me // G

    def plane(i):
        return {"seq": zi * G + lax.rem(gi + i, G)}

    def along(i):
        return {"seq": lax.rem(zi + i, Z) * G + gi}

    def other(i):
        return {"chan": lax.rem(core + i, C)}

    nxt = {"seq": lax.rem(me + 1, NSEQ)}
    prv = {"seq": lax.rem(me + NSEQ - 1, NSEQ)}

    peers = [plane(i) for i in range(1, G)] + [along(i) for i in range(1, Z)]
    peers += [other(i) for i in range(1, C)] + [nxt, prv]
    barrier = pltpu.get_barrier_semaphore()
    for peer in peers:
        pl.semaphore_signal(barrier, inc=1, device_id=peer, device_id_type=pl.DeviceIdType.MESH)

    def remote(src, dst, sems, i, device):
        return pltpu.make_async_remote_copy(
            src_ref=src, dst_ref=dst, send_sem=sems.at[0, i], recv_sem=sems.at[1, i],
            device_id=device, device_id_type=pl.DeviceIdType.MESH,
        )

    def loop(count, body):
        lax.fori_loop(0, count, lambda i, _: (body(i), None)[1], None)

    def cols(j, width=LANES):
        return pl.ds(pl.multiple_of(j * width, width), width)

    low = lax.broadcasted_iota(jnp.int32, (HW, LANES), 1) < HW

    def pair_weights(src, dst):
        def one(j):
            a = src[2 * j].astype(F32)
            b = src[2 * j + 1].astype(F32)
            ar = pltpu.roll(a, HW, 1)
            br = pltpu.roll(b, HW, 1)
            dst[j, :HW, :LANES] = jnp.where(low, a, 0.0).astype(BF16)
            dst[j, HW:, :LANES] = jnp.where(low, 0.0, br).astype(BF16)
            dst[j, :HW, LANES:] = jnp.where(low, ar, 0.0).astype(BF16)
            dst[j, HW:, LANES:] = jnp.where(low, 0.0, b).astype(BF16)
        loop(NP, one)

    def unpair(r):
        top_re, top_im = r[:HW, :LANES], r[:HW, LANES:]
        bot_re, bot_im = r[HW:, :LANES], r[HW:, LANES:]
        a = jnp.where(low, top_re, pltpu.roll(top_im, HW, 1))
        b = jnp.where(low, pltpu.roll(bot_re, HW, 1), bot_im)
        return a, b

    pl.semaphore_wait(barrier, len(peers))
    send_halo = remote(tok.at[pl.ds(T - 16, 16)], halo, s_halo, 0, nxt)
    send_halo.start()

    pair_weights(win, w_in)
    pair_weights(wout, w_out)
    if PP != NP:
        d_re[...] = jnp.zeros_like(d_re)
        d_im[...] = jnp.zeros_like(d_im)
    msg_i[pl.ds(ROWS, RI - ROWS), :] = jnp.zeros((RI - ROWS, LANES), BF16)
    if RO > ROWS:
        msg_o[pl.ds(ROWS, RO - ROWS), :] = jnp.zeros((RO - ROWS, LANES), BF16)
    tsc[...] = jnp.zeros_like(tsc)
    scale_row[...] = scale_of(rate_row[...])
    mag = jnp.exp(-rate_t[...])
    lam = (mag * jnp.cos(rot_t[...]), mag * jnp.sin(rot_t[...]))
    lam_dev = cpow(lam, T)
    lam_plane = cpow(lam_dev, G)

    def widen(j):
        pad[pl.ds(8, T), cols(j)] = tok[:, cols(j)].astype(F32)
    loop(NP, widen)
    send_halo.wait()

    def lead(j):
        rows = halo[:, cols(j)].astype(F32)[8:]
        pad[pl.ds(0, 8), cols(j)] = jnp.where(me == 0, 0.0, rows)
    loop(NP, lead)

    def forward_in(j):
        conv = taps[pl.ds(0, 1), cols(j)] * pad[pl.ds(8, T), cols(j)]
        for k in range(1, KW):
            conv = conv + taps[pl.ds(k, 1), cols(j)] * pad[pl.ds(8 - k, T), cols(j)]
        x = conv.astype(BF16)
        mixed_in[:, cols(j)] = x
        drive = dot(x, w_in[j], 1, 0)
        scale = scale_row[:, cols(j)]
        d_re[pl.ds(j, T, PP), :] = drive[:, :LANES] * scale
        d_im[pl.ds(j, T, PP), :] = drive[:, LANES:] * scale
    loop(NP, forward_in)

    zero = jnp.zeros((PP, LANES), F32)
    STEP = 8

    def tile(t):
        return pl.ds(pl.multiple_of(t * PP, PP), PP)

    def run(re, im, write):
        def steps(b, carry):
            re, im, kp = carry
            for u in range(STEP):
                t = b * STEP + u
                k = keep[t]
                cr, ci = lam[0] * k, lam[1] * k
                xr, xi = d_re[tile(t), :], d_im[tile(t), :]
                re, im = (cr * re + xr) - ci * im, (cr * im + xi) + ci * re
                kp = kp * k
                if write:
                    d_re[tile(t), :] = re
                    d_im[tile(t), :] = im
            return re, im, kp
        return lax.fori_loop(0, T // STEP, steps, (re, im, jnp.ones((8, LANES), F32)))

    def run_back(re, im, write):
        def steps(b, carry):
            re, im = carry
            for u in range(STEP):
                t = T - 1 - (b * STEP + u)
                k = keep[t]
                cr, ci = lam[0] * k, lam[1] * k
                ar, ai = d_re[tile(t), :] + re, d_im[tile(t), :] + im
                if write:
                    d_re[tile(t), :] = ar
                    d_im[tile(t), :] = ai
                re, im = cr * ar + ci * ai, cr * ai - ci * ar
            return re, im
        return lax.fori_loop(0, T // STEP, steps, (re, im))

    def put(buf, value, k):
        buf[0, :PP, :] = value[0]
        buf[0, PP:2 * PP, :] = value[1]
        buf[0, 2 * PP:, :] = k

    def entry(buf, slot):
        return (buf[slot, :PP, :], buf[slot, PP:2 * PP, :]), buf[slot, pl.ds(2 * PP, 1), :]

    def fold(buf, place, count, step, init, all_too, back):
        order = range(count - 1, -1, -1) if back else range(count)
        c, total, kt = init, (zero, zero), jnp.ones((1, LANES), F32)
        for g in order:
            e, k = entry(buf, lax.rem(place - g + count, count))
            a = (step[0] * k, step[1] * k)
            m = cmul(a, c)
            use = (g > place) if back else (g < place)
            c = (jnp.where(use, m[0] + e[0], c[0]), jnp.where(use, m[1] + e[1], c[1]))
            if all_too:
                m = cmul(a, total)
                total = (m[0] + e[0], m[1] + e[1])
                kt = kt * k
        return c, total, kt

    def plane_start(buf, sems):
        copies = [remote(buf.at[0], buf.at[i], sems, i, plane(i)) for i in range(1, G)]
        for c in copies:
            c.start()
        return copies

    def z_start(buf, sems):
        copies = [remote(buf.at[0], buf.at[i], sems, i, along(i)) for i in range(1, Z)]
        for c in copies:
            c.start()
        return copies

    def wait(copies):
        for c in copies:
            c.wait()

    end_re, end_im, kprod = run(zero, zero, False)
    put(fb1, (end_re, end_im), kprod)
    wait(plane_start(fb1, s_f1))
    _, total, kt = fold(fb1, gi, G, lam_dev, (zero, zero), True, False)
    put(fb2, total, jnp.broadcast_to(kt, (8, LANES)))
    wait(z_start(fb2, s_f2))
    c, _, _ = fold(fb2, zi, Z, lam_plane, (zero, zero), False, False)
    c, _, _ = fold(fb1, gi, G, lam_dev, c, False, False)
    run(c[0], c[1], True)

    nbuf[0] = jnp.zeros((T, LANES), F32)
    half = lax.broadcasted_iota(jnp.int32, (T, LANES), 1) < HW

    def readout(j, carry):
        sq, dt = carry
        state = jnp.concatenate(
            [d_re[pl.ds(j, T, PP), :].astype(BF16), d_im[pl.ds(j, T, PP), :].astype(BF16)], axis=1)
        s_bf[:, cols(j, 2 * LANES)] = state
        m = dot(state, w_out[j], 1, 1) + skip[:, cols(j)] * mixed_in[:, cols(j)].astype(F32)
        mixed[:, cols(j)] = m
        scaled = cot[:, cols(j)].astype(F32) * gain[:, cols(j)]
        return sq + m * m, dt + scaled * m
    wide = jnp.zeros((T, LANES), F32)
    sq, dt = lax.fori_loop(0, NP, readout, (wide, wide))
    nbuf[0] = jnp.where(half, sq + pltpu.roll(sq, HW, 1), dt + pltpu.roll(dt, HW, 1))
    copies = [remote(nbuf.at[0], nbuf.at[i], s_norm, i, other(i)) for i in range(1, C)]
    for cp in copies:
        cp.start()
    wait(copies)
    both = nbuf[0]
    for i in range(1, C):
        both = both + nbuf[i]
    sq = jnp.sum(jnp.where(half, both, 0.0), axis=1, keepdims=True)
    dt = jnp.sum(jnp.where(half, 0.0, both), axis=1, keepdims=True)
    model = W * C
    inv = lax.rsqrt(sq / model + 1e-6)
    pull = inv * inv * dt / model

    def norm_back(j):
        m = mixed[:, cols(j)]
        g = gain[:, cols(j)]
        normed_o[:, cols(j)] = (m * inv * g).astype(BF16)
        scaled = cot[:, cols(j)].astype(F32) * g
        mg = inv * (scaled - m * pull)
        mixed[:, cols(j)] = mg
        gb = mg.astype(BF16)
        g_bf[:, cols(j)] = gb
        sg = dot(gb, w_out[j], 1, 0)
        d_re[pl.ds(j, T, PP), :] = sg[:, :LANES]
        d_im[pl.ds(j, T, PP), :] = sg[:, LANES:]
    loop(NP, norm_back)

    first = run_back(zero, zero, False)
    put(bb1, first, kprod)
    b1 = plane_start(bb1, s_b1)

    def out_grads(j):
        a, b = unpair(dot(g_bf[:, cols(j)], s_bf[:, cols(j, 2 * LANES)], 0, 0))
        msg_o[cols(2 * j, HW), :] = a.astype(BF16)
        msg_o[cols(2 * j + 1, HW), :] = b.astype(BF16)
    loop(NP, out_grads)

    conj_dev = (lam_dev[0], -lam_dev[1])
    conj_plane = (lam_plane[0], -lam_plane[1])
    wait(b1)
    _, total, kt = fold(bb1, gi, G, conj_dev, (zero, zero), True, True)
    put(bb2, total, jnp.broadcast_to(kt, (8, LANES)))
    b2 = z_start(bb2, s_b2)

    def chunk(i, size):
        return pl.ds(pl.multiple_of(i * size, 16), size)

    def sum1_start(msg, rs1, sems, rows):
        size = rows // G
        copies = [remote(msg.at[chunk(lax.rem(gi + i, G), size)], rs1.at[i], sems, i, plane(i))
                  for i in range(1, G)]
        for cp in copies:
            cp.start()
        return copies

    def sum1_end(copies, msg, rs1, mid, rows):
        wait(copies)
        size = rows // G
        total = msg[chunk(gi, size), :].astype(F32)
        for i in range(1, G):
            total = total + rs1[i].astype(F32)
        mid[...] = total.astype(BF16)

    def sum2_start(mid, rs2, sems, rows):
        size = rows // NSEQ
        copies = [remote(mid.at[chunk(lax.rem(zi + i, Z), size)], rs2.at[i], sems, i, along(i))
                  for i in range(1, Z)]
        for cp in copies:
            cp.start()
        return copies

    def sum2_end(copies, mid, rs2, res, rows):
        wait(copies)
        size = rows // NSEQ
        total = mid[chunk(zi, size), :].astype(F32)
        for i in range(1, Z):
            total = total + rs2[i].astype(F32)
        res[chunk(gi * Z + zi, size), :] = total.astype(BF16)

    def gather1_start(res, sems, rows):
        part = res.at[chunk(gi * Z + zi, rows // NSEQ)]
        copies = [remote(part, part, sems, i, along(i)) for i in range(1, Z)]
        for cp in copies:
            cp.start()
        return copies

    def gather2_start(res, sems, rows):
        part = res.at[chunk(gi, rows // G)]
        copies = [remote(part, part, sems, i, plane(i)) for i in range(1, G)]
        for cp in copies:
            cp.start()
        return copies

    o1 = sum1_start(msg_o, rs1_o, s_o1, RO)
    wait(b2)
    c, _, _ = fold(bb2, zi, Z, conj_plane, (zero, zero), False, True)
    c, _, _ = fold(bb1, gi, G, conj_dev, c, False, True)
    run_back(c[0], c[1], True)

    sum1_end(o1, msg_o, rs1_o, mid_o, RO)
    o2 = sum2_start(mid_o, rs2_o, s_o2, RO)

    def backward_in(j):
        scale = scale_row[:, cols(j)]
        dg = jnp.concatenate(
            [(d_re[pl.ds(j, T, PP), :] * scale).astype(BF16),
             (d_im[pl.ds(j, T, PP), :] * scale).astype(BF16)], axis=1)
        a, b = unpair(dot(mixed_in[:, cols(j)], dg, 0, 0))
        msg_i[cols(2 * j, HW), :] = a.astype(BF16)
        msg_i[cols(2 * j + 1, HW), :] = b.astype(BF16)
        g = dot(dg, w_in[j], 1, 1) + skip[:, cols(j)] * mixed[:, cols(j)]
        ig[pl.ds(0, T), cols(j)] = g
        for k in range(KW):
            tsc[pl.ds(k * NP + j, 1), :] = jnp.sum(
                g * pad[pl.ds(8 - k, T), cols(j)], axis=0, keepdims=True)
    loop(NP, backward_in)
    msg_i[pl.ds(ROWS, tsc.shape[0]), :] = tsc[...].astype(BF16)
    send_ig = remote(ig.at[pl.ds(0, 8)], ihalo, s_halo, 1, prv)
    send_ig.start()
    i1 = sum1_start(msg_i, rs1_i, s_i1, RI)

    sum2_end(o2, mid_o, rs2_o, res_o, RO)
    o3 = gather1_start(res_o, s_o3, RO)
    send_ig.wait()

    def token_grads(j):
        ig[pl.ds(T, 8), cols(j)] = jnp.where(me == NSEQ - 1, 0.0, ihalo[:, cols(j)])
        g = taps[pl.ds(0, 1), cols(j)] * ig[pl.ds(0, T), cols(j)]
        for k in range(1, KW):
            g = g + taps[pl.ds(k, 1), cols(j)] * ig[pl.ds(k, T), cols(j)]
        tg_o[:, cols(j)] = g.astype(BF16)
    loop(NP, token_grads)

    sum1_end(i1, msg_i, rs1_i, mid_i, RI)
    i2 = sum2_start(mid_i, rs2_i, s_i2, RI)
    wait(o3)
    o4 = gather2_start(res_o, s_o4, RO)
    sum2_end(i2, mid_i, rs2_i, res_i, RI)
    i3 = gather1_start(res_i, s_i3, RI)

    def widen_out(res, out):
        def one(h):
            out[h] = res[cols(h, HW), :].astype(F32)
        loop(ROWS // HW, one)

    wait(i3)
    i4 = gather2_start(res_i, s_i4, RI)
    wait(o4)
    widen_out(res_o, out_o)
    wait(i4)
    widen_out(res_i, in_o)
    tsc[...] = res_i[pl.ds(ROWS, tsc.shape[0]), :].astype(F32)

    def put_taps(j):
        for k in range(KW):
            taps_o[pl.ds(k, 1), cols(j)] = tsc[pl.ds(k * NP + j, 1), :]
    loop(NP, put_taps)


def up(value, unit):
    return -(-value // unit) * unit


def per_device(num_seq, num_chan, tokens, conv_taps, log_rate, rotation, in_proj, out_proj,
               skip_gain, norm_gain, retention, cotangent):
    T, W = tokens.shape
    KW = conv_taps.shape[0]
    NH, HW, K2 = in_proj.shape
    NP = NH // 2
    PP = up(NP, 8)
    G = 1
    while G * G < num_seq:
        G *= 2
    Z = num_seq // G
    ROWS = NH * HW
    TP = up(KW * NP, 16)
    RO = up(ROWS, num_seq * 16)
    RI = up(ROWS + TP, num_seq * 16)
    dims = (T, W, NP, PP, KW, HW, G, Z, num_chan, num_seq, ROWS, RO, RI)

    def tiled(x):
        x = x.reshape(NP, LANES)
        return jnp.pad(x, ((0, PP - NP), (0, 0))) if PP != NP else x

    row = lambda x: x.reshape(1, W)
    vm = pl.BlockSpec(memory_space=pltpu.VMEM)
    sm = pl.BlockSpec(memory_space=pltpu.SMEM)
    V = pltpu.VMEM
    M = 2 * PP + 8
    sem = lambda n: pltpu.SemaphoreType.DMA((2, n))

    def bufs(rows):
        return [V((rows, LANES), BF16), V((G, rows // G, LANES), BF16), V((rows // G, LANES), BF16),
                V((Z, rows // num_seq, LANES), BF16), V((rows, LANES), BF16)]

    scratch = [
        V((T + 8, W), F32), V((T, W), BF16), V((T * PP, LANES), F32), V((T * PP, LANES), F32),
        V((T, 2 * W), BF16), V((T, W), F32), V((T, W), BF16), V((T + 8, W), F32),
        V((NP, 2 * HW, 2 * LANES), BF16), V((NP, 2 * HW, 2 * LANES), BF16), V((1, W), F32),
        V((TP, LANES), F32), V((16, W), BF16), V((8, W), F32),
        V((num_chan, T, LANES), F32),
        V((G, M, LANES), F32), V((Z, M, LANES), F32), V((G, M, LANES), F32), V((Z, M, LANES), F32),
        *bufs(RO), *bufs(RI),
        sem(2), sem(num_chan), sem(G), sem(Z), sem(G), sem(Z),
        sem(G), sem(Z), sem(Z), sem(G), sem(G), sem(Z), sem(Z), sem(G),
    ]
    S = jax.ShapeDtypeStruct
    return pl.pallas_call(
        functools.partial(kernel, dims),
        out_shape=(S((T, W), BF16), S((T, W), BF16), S((NH, HW, K2), F32), S((NH, HW, K2), F32),
                   S((KW, W), F32)),
        in_specs=[vm] * 10 + [sm],
        out_specs=(vm,) * 5,
        scratch_shapes=scratch,
        compiler_params=pltpu.CompilerParams(
            collective_id=0, has_side_effects=True, vmem_limit_bytes=48 * 1024 * 1024),
    )(tokens, conv_taps, row(log_rate), tiled(log_rate), tiled(rotation), in_proj, out_proj,
      row(skip_gain), row(norm_gain), cotangent, retention)


def solution(mesh):
    in_specs = (
        P("seq", "chan"), P(None, "chan"), P("chan"), P("chan"), P("chan", None, None),
        P("chan", None, None), P("chan"), P("chan"), P("seq"), P("seq", "chan"),
    )
    out_specs = (
        P("seq", "chan"), P("seq", "chan"), P("chan", None, None), P("chan", None, None),
        P(None, "chan"),
    )
    body = functools.partial(per_device, mesh.shape["seq"], mesh.shape["chan"])
    return jax.shard_map(body, mesh=mesh, in_specs=in_specs, out_specs=out_specs, check_vma=False)
```

time: 688 us -> 85.8 us (0.12); the launches traced: 680 us -> 85.3 us
  blocking collectives: 365 us -> 0 us
  local copies, waits for them, and re-layouts: 178 us -> 11.8 us
  Pallas kernels: 0 us -> 72.8 us
  other arithmetic: 68 us -> 0 us
  waiting for transfers between devices: 33.2 us -> 0 us
  between operations: 15.4 us -> 0.67 us
  matrix products: 11.6 us -> 0 us
  starting transfers between devices: 6.95 us -> 0 us
    all_gather x7 -> x0, blocking collectives: 287 us -> none  [carried_in(): gathered = jax.tree.map(lambda a: lax.all_gather(a, axis), part)]
    psum x2 -> x0, blocking collectives: 78.1 us -> none  [the longest x1 75.7 us: per_device(): lax.psum((in_grad, out_grad, taps_grad), 'seq')]
    pallas_call x0 -> x1, Pallas kernels: none -> 72.8 us  [per_device(): pl.pallas_call(functools.partial(kernel, dims), out_shape=(S((T, W), BF16...]
    mul x22 -> x0, local copies, waits for them, and re-layouts: 42.4 us -> none  [the longest x6 12.8 us: linear_run(): pre_re = growth * (blk_re * cosine + blk_im * sine)]
    rev x4 -> x0, local copies, waits for them, and re-layouts: 35.9 us -> none  [the longest x1 9.17 us: per_device(): grad_re = state_grad[:, :, :state_size].reshape(seq_len, num_cols)[::-1]]
    psum x1 -> x0, waiting for transfers between devices: 33.2 us -> none  [per_device(): lax.psum((in_grad, out_grad, taps_grad), 'seq')]
    reshape x8 -> x0, local copies, waits for them, and re-layouts: 24.4 us -> none  [the longest x2 7.3 us: per_device(): projected[:, :, state_size:].reshape(seq_len, num_cols) * in_scale]
    another operation x13 -> x0, other arithmetic: 15.8 us -> none
  transfers between devices with their start and end apart: 3 -> 0, of which waited for: 1 -> 0; matrix products, arithmetic and copies ran while one was open for 12% -> 0% of each run, Pallas kernels for 0% -> 0%
where the time goes in v1:
time: 85.8 us; the launch traced here: 85.3 us
  Pallas kernels  72.8 us (85%)
  local copies, waits for them, and re-layouts  11.8 us (14%)
    pallas_call x1, Pallas kernels, per_device(): pl.pallas_call(functools.partial(kernel, dims), out_shape=(S((T, W), BF16...  72.8 us
    unnamed x25, local copies, waits for them, and re-layouts  11.8 us

profile of v1, /device:TPU:0, one launch (start us, length us, event | category | flops | bytes accessed | tf_op | source)
XLA Modules:
  0.0 85.3 jit_solution(3177518370253923340)
XLA Ops:
  0.6 0.0 copy-start.5
  0.6 0.0 copy-start.9
  0.7 0.7 copy-done.5
  1.3 0.0 copy-done.9
  1.3 0.0 copy-start
  1.3 1.0 %copy-done = bf16[128,2048]{1,0:T(8,128)(2,1)S(1)} copy-done((bf16[128,2048]{1,0:T(8,128)(2,1)S(1)}, bf16[128,2048]{1,0:T(8,128)(2,1)}, u32[]{:S(2)}) %copy-start) | copy-done | bytes 524312
  2.4 0.0 copy-start.1
  2.4 1.0 %copy-done.1 = bf16[32,64,128]{2,1,0:T(8,128)(2,1)S(1)} copy-done((bf16[32,64,128]{2,1,0:T(8,128)(2,1)S(1)}, bf16[32,64,128]{2,1,0:T(8,128)(2,1)}, u32[]{:S(2)}) %copy-start.1) | copy-done | bytes 524312
  3.4 0.0 copy-start.2
  3.4 1.0 %copy-done.2 = bf16[32,64,128]{2,1,0:T(8,128)(2,1)S(1)} copy-done((bf16[32,64,128]{2,1,0:T(8,128)(2,1)S(1)}, bf16[32,64,128]{2,1,0:T(8,128)(2,1)}, u32[]{:S(2)}) %copy-start.2) | copy-done | bytes 524312
  4.5 0.0 copy-start.3
  4.5 1.0 %copy-done.3 = bf16[128,2048]{1,0:T(8,128)(2,1)S(1)} copy-done((bf16[128,2048]{1,0:T(8,128)(2,1)S(1)}, bf16[128,2048]{1,0:T(8,128)(2,1)}, u32[]{:S(2)}) %copy-start.3) | copy-done | bytes 524312
  5.5 0.0 copy-start.4
  5.5 0.8 copy-done.4
  6.3 0.0 copy-start.6
  6.3 0.7 copy-done.6
  7.0 0.0 copy-start.7
  7.0 0.7 copy-done.7
  7.7 0.0 copy-start.8
  7.7 0.7 copy-done.8
  8.4 72.8 %shard_map.137 = (bf16[128,2048]{1,0:T(8,128)(2,1)S(1)}, bf16[128,2048]{1,0:T(8,128)(2,1)S(1)}, f32[32,64,128]{2,1,0:T(8,128)S(1)}, f32[32,64,128]{2,1,0:T(8,128)S(1)}, f32[4,2048]{1,0:T(4,128)S(1)}) custom-call(bf16[128,2048]{1,0:T(8,128)(2,1)S(1)} %copy-done, f32[4,2048]{1,0:T(4,128)S(1)} %copy-done.4, f32[1,2048]{1,0:T(1,128)S(1)} %bitcast.5, ...), custom_call_target="tpu_custom_call" | custom-call | tf_op jit(solution)/shard_map/pallas_call | solution.py:453
  81.2 0.8 copy.20
  82.0 0.8 copy.21
  82.7 1.0 %copy.22 = f32[32,64,128]{2,1,0:T(8,128)} copy(f32[32,64,128]{2,1,0:T(8,128)S(1)} %get-tuple-element.12) | data formatting | bytes 2097152
  83.7 1.0 %copy.23 = f32[32,64,128]{2,1,0:T(8,128)} copy(f32[32,64,128]{2,1,0:T(8,128)S(1)} %get-tuple-element.13) | data formatting | bytes 2097152
  84.7 0.6 copy.24
Async XLA Ops:
  0.6 0.7 copy-start.5
  0.6 0.7 copy-start.9
  1.3 1.0 %copy-start = (bf16[128,2048]{1,0:T(8,128)(2,1)S(1)}, bf16[128,2048]{1,0:T(8,128)(2,1)}, u32[]{:S(2)}) copy-start(bf16[128,2048]{1,0:T(8,128)(2,1)} %refs_0_.1) | copy-start | bytes 1572868
  2.4 1.0 %copy-start.1 = (bf16[32,64,128]{2,1,0:T(8,128)(2,1)S(1)}, bf16[32,64,128]{2,1,0:T(8,128)(2,1)}, u32[]{:S(2)}) copy-start(bf16[32,64,128]{2,1,0:T(8,128)(2,1)} %refs_5_.1) | copy-start | bytes 1572868
  3.4 1.0 %copy-start.2 = (bf16[32,64,128]{2,1,0:T(8,128)(2,1)S(1)}, bf16[32,64,128]{2,1,0:T(8,128)(2,1)}, u32[]{:S(2)}) copy-start(bf16[32,64,128]{2,1,0:T(8,128)(2,1)} %refs_6_.1) | copy-start | bytes 1572868
  4.5 1.0 %copy-start.3 = (bf16[128,2048]{1,0:T(8,128)(2,1)S(1)}, bf16[128,2048]{1,0:T(8,128)(2,1)}, u32[]{:S(2)}) copy-start(bf16[128,2048]{1,0:T(8,128)(2,1)} %refs_9_.1) | copy-start | bytes 1572868
  5.5 0.8 copy-start.4
  6.3 0.7 copy-start.6
  7.0 0.7 copy-start.7
  7.7 0.7 copy-start.8

commit v2 on v1

--- a/solution.py
+++ b/solution.py
@@ -38,11 +38,12 @@
 
 
 def kernel(dims, *refs):
-    (tok, taps, rate_row, rate_t, rot_t, win, wout, skip, gain, cot, keep,
-     normed_o, tg_o, in_o, out_o, taps_o,
+    (tok_h, taps_h, rate_row_h, rate_t_h, rot_t_h, win_h, wout_h, skip_h, gain_h, cot_h, keep,
+     normed_o, tg_o, res_o, res_i, taps_o,
+     tok, taps, rate_row, rate_t, rot_t, win, wout, skip, gain, cot, s_in,
      pad, mixed_in, d_re, d_im, s_bf, mixed, g_bf, ig, w_in, w_out, scale_row, tsc, halo, ihalo,
-     nbuf, fb1, fb2, bb1, bb2, msg_o, rs1_o, mid_o, rs2_o, res_o,
-     msg_i, rs1_i, mid_i, rs2_i, res_i,
+     nbuf, fb1, fb2, bb1, bb2, msg_o, rs1_o, mid_o, rs2_o,
+     msg_i, rs1_i, mid_i, rs2_i,
      s_halo, s_norm, s_f1, s_f2, s_b1, s_b2, s_o1, s_o2, s_o3, s_o4, s_i1, s_i2, s_i3, s_i4) = refs
     T, W, NP, PP, KW, HW, G, Z, C, NSEQ, ROWS, RO, RI = dims
     me = lax.axis_index("seq")
@@ -68,6 +69,13 @@
     for peer in peers:
         pl.semaphore_signal(barrier, inc=1, device_id=peer, device_id_type=pl.DeviceIdType.MESH)
 
+    pairs = [(tok_h, tok), (win_h, win), (taps_h, taps), (rate_row_h, rate_row),
+             (rate_t_h, rate_t), (rot_t_h, rot_t), (wout_h, wout), (skip_h, skip),
+             (gain_h, gain), (cot_h, cot)]
+    loads = [pltpu.make_async_copy(src, dst, s_in.at[i]) for i, (src, dst) in enumerate(pairs)]
+    for cp in loads:
+        cp.start()
+
     def remote(src, dst, sems, i, device):
         return pltpu.make_async_remote_copy(
             src_ref=src, dst_ref=dst, send_sem=sems.at[0, i], recv_sem=sems.at[1, i],
@@ -75,7 +83,12 @@
         )
 
     def loop(count, body):
-        lax.fori_loop(0, count, lambda i, _: (body(i), None)[1], None)
+        unroll = 4 if count % 4 == 0 else 1
+
+        def several(i, _):
+            for u in range(unroll):
+                body(i * unroll + u)
+        lax.fori_loop(0, count // unroll, several, None)
 
     def cols(j, width=LANES):
         return pl.ds(pl.multiple_of(j * width, width), width)
@@ -101,24 +114,22 @@
         b = jnp.where(low, pltpu.roll(bot_re, HW, 1), bot_im)
         return a, b
 
-    pl.semaphore_wait(barrier, len(peers))
-    send_halo = remote(tok.at[pl.ds(T - 16, 16)], halo, s_halo, 0, nxt)
-    send_halo.start()
-
+    for cp in loads[1:6]:
+        cp.wait()
     pair_weights(win, w_in)
-    pair_weights(wout, w_out)
-    if PP != NP:
-        d_re[...] = jnp.zeros_like(d_re)
-        d_im[...] = jnp.zeros_like(d_im)
-    msg_i[pl.ds(ROWS, RI - ROWS), :] = jnp.zeros((RI - ROWS, LANES), BF16)
-    if RO > ROWS:
-        msg_o[pl.ds(ROWS, RO - ROWS), :] = jnp.zeros((RO - ROWS, LANES), BF16)
-    tsc[...] = jnp.zeros_like(tsc)
     scale_row[...] = scale_of(rate_row[...])
     mag = jnp.exp(-rate_t[...])
     lam = (mag * jnp.cos(rot_t[...]), mag * jnp.sin(rot_t[...]))
     lam_dev = cpow(lam, T)
     lam_plane = cpow(lam_dev, G)
+    pl.semaphore_wait(barrier, len(peers))
+    send_halo = remote(tok_h.at[pl.ds(T - 16, 16)], halo, s_halo, 0, nxt)
+    send_halo.start()
+    loads[0].wait()
+
+    if PP != NP:
+        d_re[...] = jnp.zeros_like(d_re)
+        d_im[...] = jnp.zeros_like(d_im)
 
     def widen(j):
         pad[pl.ds(8, T), cols(j)] = tok[:, cols(j)].astype(F32)
@@ -220,7 +231,15 @@
 
     end_re, end_im, kprod = run(zero, zero, False)
     put(fb1, (end_re, end_im), kprod)
-    wait(plane_start(fb1, s_f1))
+    f1 = plane_start(fb1, s_f1)
+    for cp in loads[6:]:
+        cp.wait()
+    pair_weights(wout, w_out)
+    msg_i[pl.ds(ROWS, RI - ROWS), :] = jnp.zeros((RI - ROWS, LANES), BF16)
+    if RO > ROWS:
+        msg_o[pl.ds(ROWS, RO - ROWS), :] = jnp.zeros((RO - ROWS, LANES), BF16)
+    tsc[...] = jnp.zeros_like(tsc)
+    wait(f1)
     _, total, kt = fold(fb1, gi, G, lam_dev, (zero, zero), True, False)
     put(fb2, total, jnp.broadcast_to(kt, (8, LANES)))
     wait(z_start(fb2, s_f2))
@@ -228,10 +247,9 @@
     c, _, _ = fold(fb1, gi, G, lam_dev, c, False, False)
     run(c[0], c[1], True)
 
-    nbuf[0] = jnp.zeros((T, LANES), F32)
     half = lax.broadcasted_iota(jnp.int32, (T, LANES), 1) < HW
 
-    def readout(j, carry):
+    def readout_one(j, carry):
         sq, dt = carry
         state = jnp.concatenate(
             [d_re[pl.ds(j, T, PP), :].astype(BF16), d_im[pl.ds(j, T, PP), :].astype(BF16)], axis=1)
@@ -240,8 +258,14 @@
         mixed[:, cols(j)] = m
         scaled = cot[:, cols(j)].astype(F32) * gain[:, cols(j)]
         return sq + m * m, dt + scaled * m
+    runs = 4 if NP % 4 == 0 else 1
+
+    def readout(i, carry):
+        for u in range(runs):
+            carry = readout_one(i * runs + u, carry)
+        return carry
     wide = jnp.zeros((T, LANES), F32)
-    sq, dt = lax.fori_loop(0, NP, readout, (wide, wide))
+    sq, dt = lax.fori_loop(0, NP // runs, readout, (wide, wide))
     nbuf[0] = jnp.where(half, sq + pltpu.roll(sq, HW, 1), dt + pltpu.roll(dt, HW, 1))
     copies = [remote(nbuf.at[0], nbuf.at[i], s_norm, i, other(i)) for i in range(1, C)]
     for cp in copies:
@@ -341,9 +365,6 @@
     c, _, _ = fold(bb2, zi, Z, conj_plane, (zero, zero), False, True)
     c, _, _ = fold(bb1, gi, G, conj_dev, c, False, True)
     run_back(c[0], c[1], True)
-
-    sum1_end(o1, msg_o, rs1_o, mid_o, RO)
-    o2 = sum2_start(mid_o, rs2_o, s_o2, RO)
 
     def backward_in(j):
         scale = scale_row[:, cols(j)]
@@ -363,6 +384,8 @@
     send_ig = remote(ig.at[pl.ds(0, 8)], ihalo, s_halo, 1, prv)
     send_ig.start()
     i1 = sum1_start(msg_i, rs1_i, s_i1, RI)
+    sum1_end(o1, msg_o, rs1_o, mid_o, RO)
+    o2 = sum2_start(mid_o, rs2_o, s_o2, RO)
 
     sum2_end(o2, mid_o, rs2_o, res_o, RO)
     o3 = gather1_start(res_o, s_o3, RO)
@@ -383,23 +406,37 @@
     sum2_end(i2, mid_i, rs2_i, res_i, RI)
     i3 = gather1_start(res_i, s_i3, RI)
 
-    def widen_out(res, out):
-        def one(h):
-            out[h] = res[cols(h, HW), :].astype(F32)
-        loop(ROWS // HW, one)
-
     wait(i3)
     i4 = gather2_start(res_i, s_i4, RI)
     wait(o4)
-    widen_out(res_o, out_o)
     wait(i4)
-    widen_out(res_i, in_o)
     tsc[...] = res_i[pl.ds(ROWS, tsc.shape[0]), :].astype(F32)
 
     def put_taps(j):
         for k in range(KW):
             taps_o[pl.ds(k, 1), cols(j)] = tsc[pl.ds(k * NP + j, 1), :]
     loop(NP, put_taps)
+
+
+def finish(dims, normed, tg, res_o, res_i, taps, normed_h, tg_h, in_h, out_h, taps_h,
+           wide_o, wide_i, sems):
+    NH, HW, PARTS = dims
+    copies = []
+
+    def put(src, dst):
+        copies.append(pltpu.make_async_copy(src, dst, sems.at[len(copies)]))
+        copies[-1].start()
+    put(normed, normed_h)
+    put(tg, tg_h)
+    put(taps, taps_h)
+    step = NH // PARTS
+    for res, wide, out in ((res_o, wide_o, out_h), (res_i, wide_i, in_h)):
+        for p in range(PARTS):
+            for h in range(p * step, (p + 1) * step):
+                wide[h] = res[pl.ds(h * HW, HW), :].astype(F32)
+            put(wide.at[pl.ds(p * step, step)], out.at[pl.ds(p * step, step)])
+    for cp in copies:
+        cp.wait()
 
 
 def up(value, unit):
@@ -430,15 +467,19 @@
     row = lambda x: x.reshape(1, W)
     vm = pl.BlockSpec(memory_space=pltpu.VMEM)
     sm = pl.BlockSpec(memory_space=pltpu.SMEM)
+    hb = pl.BlockSpec(memory_space=pltpu.HBM)
     V = pltpu.VMEM
     M = 2 * PP + 8
     sem = lambda n: pltpu.SemaphoreType.DMA((2, n))
 
     def bufs(rows):
         return [V((rows, LANES), BF16), V((G, rows // G, LANES), BF16), V((rows // G, LANES), BF16),
-                V((Z, rows // num_seq, LANES), BF16), V((rows, LANES), BF16)]
+                V((Z, rows // num_seq, LANES), BF16)]
 
     scratch = [
+        V((T, W), BF16), V((KW, W), F32), V((1, W), F32), V((PP, LANES), F32), V((PP, LANES), F32),
+        V((NH, HW, K2), BF16), V((NH, HW, K2), BF16), V((1, W), F32), V((1, W), F32), V((T, W), BF16),
+        pltpu.SemaphoreType.DMA((10,)),
         V((T + 8, W), F32), V((T, W), BF16), V((T * PP, LANES), F32), V((T * PP, LANES), F32),
         V((T, 2 * W), BF16), V((T, W), F32), V((T, W), BF16), V((T + 8, W), F32),
         V((NP, 2 * HW, 2 * LANES), BF16), V((NP, 2 * HW, 2 * LANES), BF16), V((1, W), F32),
@@ -450,17 +491,28 @@
         sem(G), sem(Z), sem(Z), sem(G), sem(G), sem(Z), sem(Z), sem(G),
     ]
     S = jax.ShapeDtypeStruct
-    return pl.pallas_call(
+    normed, tg, res_o, res_i, taps = pl.pallas_call(
         functools.partial(kernel, dims),
-        out_shape=(S((T, W), BF16), S((T, W), BF16), S((NH, HW, K2), F32), S((NH, HW, K2), F32),
+        out_shape=(S((T, W), BF16), S((T, W), BF16), S((RO, LANES), BF16), S((RI, LANES), BF16),
                    S((KW, W), F32)),
-        in_specs=[vm] * 10 + [sm],
+        in_specs=[hb] * 10 + [sm],
         out_specs=(vm,) * 5,
         scratch_shapes=scratch,
         compiler_params=pltpu.CompilerParams(
             collective_id=0, has_side_effects=True, vmem_limit_bytes=48 * 1024 * 1024),
     )(tokens, conv_taps, row(log_rate), tiled(log_rate), tiled(rotation), in_proj, out_proj,
       row(skip_gain), row(norm_gain), cotangent, retention)
+    parts = 4
+    return pl.pallas_call(
+        functools.partial(finish, (NH, HW, parts)),
+        out_shape=(S((T, W), BF16), S((T, W), BF16), S((NH, HW, K2), F32), S((NH, HW, K2), F32),
+                   S((KW, W), F32)),
+        in_specs=[vm] * 5,
+        out_specs=(hb,) * 5,
+        scratch_shapes=[V((NH, HW, K2), F32), V((NH, HW, K2), F32),
+                        pltpu.SemaphoreType.DMA((3 + 2 * parts,))],
+        compiler_params=pltpu.CompilerParams(vmem_limit_bytes=16 * 1024 * 1024),
+    )(normed, tg, res_o, res_i, taps)
 
 
 def solution(mesh):

time: 85.8 us -> 70.2 us (0.82)
  Pallas kernels: 72.8 us -> 61.3 us
  local copies, waits for them, and re-layouts: 11.8 us -> 7.7 us
    pallas_call x1, Pallas kernels: 72.8 us -> 59.5 us  [per_device(): pl.pallas_call(functools.partial(kernel, dims), out_shape=(S((T, W), BF16...]
    unnamed x25 -> x20, local copies, waits for them, and re-layouts: 11.8 us -> 7.7 us
    pallas_call x0 -> x1, Pallas kernels: none -> 1.76 us  [per_device(): pl.pallas_call(functools.partial(finish, (NH, HW, parts)), out_shape=(S((...]
where the time goes in v2:
time: 70.2 us; the launch traced here: 69.7 us
  Pallas kernels  61.3 us (87%)
  local copies, waits for them, and re-layouts  7.7 us (11%)
    pallas_call x1, Pallas kernels, per_device(): pl.pallas_call(functools.partial(kernel, dims), out_shape=(S((T, W), BF16...  59.5 us
    unnamed x20, local copies, waits for them, and re-layouts  7.7 us
    pallas_call x1, Pallas kernels, per_device(): pl.pallas_call(functools.partial(finish, (NH, HW, parts)), out_shape=(S((...  1.76 us

profile of v2, /device:TPU:0, one launch (start us, length us, event | category | flops | bytes accessed | tf_op | source)
XLA Modules:
  0.0 69.7 jit_solution(3282526009311213979)
XLA Ops:
  0.6 0.0 copy-start.5
  0.6 0.0 copy-start.9
  0.7 0.7 copy-done.5
  1.3 0.0 copy-done.9
  1.3 0.0 copy-start
  1.3 1.0 %copy-done = bf16[128,2048]{1,0:T(8,128)(2,1)S(1)} copy-done((bf16[128,2048]{1,0:T(8,128)(2,1)S(1)}, bf16[128,2048]{1,0:T(8,128)(2,1)}, u32[]{:S(2)}) %copy-start) | copy-done | bytes 524312
  2.4 0.0 copy-start.1
  2.4 1.0 %copy-done.1 = bf16[32,64,128]{2,1,0:T(8,128)(2,1)S(1)} copy-done((bf16[32,64,128]{2,1,0:T(8,128)(2,1)S(1)}, bf16[32,64,128]{2,1,0:T(8,128)(2,1)}, u32[]{:S(2)}) %copy-start.1) | copy-done | bytes 524312
  3.4 0.0 copy-start.2
  3.4 1.0 %copy-done.2 = bf16[32,64,128]{2,1,0:T(8,128)(2,1)S(1)} copy-done((bf16[32,64,128]{2,1,0:T(8,128)(2,1)S(1)}, bf16[32,64,128]{2,1,0:T(8,128)(2,1)}, u32[]{:S(2)}) %copy-start.2) | copy-done | bytes 524312
  4.5 0.0 copy-start.3
  4.5 1.0 %copy-done.3 = bf16[128,2048]{1,0:T(8,128)(2,1)S(1)} copy-done((bf16[128,2048]{1,0:T(8,128)(2,1)S(1)}, bf16[128,2048]{1,0:T(8,128)(2,1)}, u32[]{:S(2)}) %copy-start.3) | copy-done | bytes 524312
  5.5 0.0 copy-start.4
  5.5 0.8 %copy-done.4 = f32[4,2048]{1,0:T(4,128)S(1)} copy-done((f32[4,2048]{1,0:T(4,128)S(1)}, f32[4,2048]{1,0:T(4,128)}, u32[]{:S(2)}) %copy-start.4) | copy-done | bytes 32792
  6.3 0.0 copy-start.6
  6.3 0.7 copy-done.6
  7.0 0.0 copy-start.7
  7.0 0.7 copy-done.7
  7.7 0.0 copy-start.8
  7.7 0.7 copy-done.8
  8.4 59.5 %shard_map.137 = (bf16[128,2048]{1,0:T(8,128)(2,1)S(1)}, bf16[128,2048]{1,0:T(8,128)(2,1)S(1)}, bf16[2048,128]{1,0:T(8,128)(2,1)S(1)}, bf16[2304,128]{1,0:T(8,128)(2,1)S(1)}, f32[4,2048]{1,0:T(4,128)S(1)}) custom-call(bf16[128,2048]{1,0:T(8,128)(2,1)S(1)} %copy-done, f32[4,2048]{1,0:T(4,128)S(1)} %copy-done.4, f32[1,2048]{1,0:T(1,128)S(1)} %bitcast.5, ...), custom_call_target="tpu_custom_call" | custom-call | tf_op jit(solution)/shard_map/pallas_call | solution.py:494
  67.9 1.8 %shard_map.138 = (bf16[128,2048]{1,0:T(8,128)(2,1)}, bf16[128,2048]{1,0:T(8,128)(2,1)}, f32[32,64,128]{2,1,0:T(8,128)}, f32[32,64,128]{2,1,0:T(8,128)}, f32[4,2048]{1,0:T(4,128)}) custom-call(bf16[128,2048]{1,0:T(8,128)(2,1)S(1)} %get-tuple-element.10.normed, bf16[128,2048]{1,0:T(8,128)(2,1)S(1)} %get-tuple-element.11.tg, ...), custom_call_target="tpu_custom_call" | custom-call | tf_op jit(solution)/shard_map/pallas_call | solution.py:506
Async XLA Ops:
  0.6 0.7 %copy-start.5 = (f32[2048]{0:T(1024)S(1)}, f32[2048]{0:T(1024)}, u32[]{:S(2)}) copy-start(f32[2048]{0:T(1024)} %param.12) | copy-start | bytes 24580
  0.6 0.7 copy-start.9
  1.3 1.0 %copy-start = (bf16[128,2048]{1,0:T(8,128)(2,1)S(1)}, bf16[128,2048]{1,0:T(8,128)(2,1)}, u32[]{:S(2)}) copy-start(bf16[128,2048]{1,0:T(8,128)(2,1)} %refs_0_.1) | copy-start | bytes 1572868
  2.4 1.0 %copy-start.1 = (bf16[32,64,128]{2,1,0:T(8,128)(2,1)S(1)}, bf16[32,64,128]{2,1,0:T(8,128)(2,1)}, u32[]{:S(2)}) copy-start(bf16[32,64,128]{2,1,0:T(8,128)(2,1)} %refs_5_.1) | copy-start | bytes 1572868
  3.4 1.0 %copy-start.2 = (bf16[32,64,128]{2,1,0:T(8,128)(2,1)S(1)}, bf16[32,64,128]{2,1,0:T(8,128)(2,1)}, u32[]{:S(2)}) copy-start(bf16[32,64,128]{2,1,0:T(8,128)(2,1)} %refs_6_.1) | copy-start | bytes 1572868
  4.5 1.0 %copy-start.3 = (bf16[128,2048]{1,0:T(8,128)(2,1)S(1)}, bf16[128,2048]{1,0:T(8,128)(2,1)}, u32[]{:S(2)}) copy-start(bf16[128,2048]{1,0:T(8,128)(2,1)} %refs_9_.1) | copy-start | bytes 1572868
  5.5 0.8 %copy-start.4 = (f32[4,2048]{1,0:T(4,128)S(1)}, f32[4,2048]{1,0:T(4,128)}, u32[]{:S(2)}) copy-start(f32[4,2048]{1,0:T(4,128)} %refs_1_.1) | copy-start | bytes 98308
  6.3 0.7 %copy-start.6 = (f32[2048]{0:T(1024)S(1)}, f32[2048]{0:T(1024)}, u32[]{:S(2)}) copy-start(f32[2048]{0:T(1024)} %param.13) | copy-start | bytes 24580
  7.0 0.7 %copy-start.7 = (f32[2048]{0:T(1024)S(1)}, f32[2048]{0:T(1024)}, u32[]{:S(2)}) copy-start(f32[2048]{0:T(1024)} %param.16) | copy-start | bytes 24580
  7.7 0.7 %copy-start.8 = (f32[2048]{0:T(1024)S(1)}, f32[2048]{0:T(1024)}, u32[]{:S(2)}) copy-start(f32[2048]{0:T(1024)} %param.17) | copy-start | bytes 24580
